TPU v7x, 128 devices: a whole 4x4x4 slice. The times are simulated.
128 devices in a mesh: dp: 4 (over x), ctx: 32 (over y, z, core).
Axes of the slice: x: 4, y: 4, z: 4, core: 2. Of those that a mesh axis runs over, the one named last changes fastest.
Arguments:
- query_states: bfloat16 [4, 4096, 2048], P('dp', 'ctx'), may hold values from -24 to 24
- key_states: bfloat16 [4, 4096, 1024], P('dp', 'ctx'), may hold values from -6 to 6
- value_states: bfloat16 [4, 4096, 1024], P('dp', 'ctx'), may hold values from -6 to 6
- out_grads: bfloat16 [4, 4096, 2048], P('dp', 'ctx'), may hold values from -6 to 6
- image_counts: int32 [4], P('dp'), may hold values from 256 to 2048, as said below
- prefix_lengths: int32 [4], P('dp'), may hold values from 257 to 3072, as said below
- encoder_owner: int32 [4], replicated, may hold values from 0 to 3, each once
- key_weight: bfloat16 [4608, 1024], replicated, may hold values from -0.09375 to 0.09375
- value_weight: bfloat16 [4608, 1024], replicated, may hold values from -0.09375 to 0.09375
- norm_scale: float32 [4608], P('dp'), may hold values from 0.5 to 2
- image_embed: bfloat16 [4, 2048, 4608], P(None, 'ctx', 'dp'), may hold values from -1200 to 1200
Outputs:
- query_grads: bfloat16 [4, 4096, 2048], P('dp', 'ctx')
- key_grads: bfloat16 [4, 4096, 1024], P('dp', 'ctx')
- value_grads: bfloat16 [4, 4096, 1024], P('dp', 'ctx')
- image_grads: float32 [4, 2048, 4608], P(None, 'ctx', 'dp')
Inputs may be any that keep to these rules, and one draw needn't show every extreme that they name: `image_counts`: in every draw one sample has exactly 2048 image tokens and another exactly 256. `prefix_lengths`: each is at least one more than its sample's image_counts; in every draw one reaches 3072.
All inputs are finite; a program needn't handle non-finite values.
Results may differ from a plain program's by a relative error of at most 0.02.
Values may be sent and summed in bfloat16 or wider, within the bound.
No kernel may reach another device: no remote copies, remote signals or barrier semaphores. Data moves between devices by JAX's collectives and lax.ppermute only.
A program may use at most 192 MiB of HBM per device.

v0:
```python
import functools
import math

import jax
import jax.numpy as jnp
from jax import lax
from jax.experimental import pallas as pl
from jax.experimental.pallas import tpu as pltpu
from jax.sharding import Mesh, PartitionSpec as P

D = 4608
HD = 128
KVH = 8
TOK = 128
SLOTS = 64
NDP = 4
FS = D // NDP
SEG = 512
NSEG = 8

score_scale = 144.0 ** (-0.5)
soft_cap = 50.0
norm_eps = 1e-06
tanh_scale = score_scale / soft_cap
exp2_scale = soft_cap * math.log2(math.e)

f32 = jnp.float32
bf16 = jnp.bfloat16
VM = pl.BlockSpec(memory_space=pltpu.VMEM)
ANY = pl.BlockSpec(memory_space=pl.ANY)
SM = pl.BlockSpec(memory_space=pltpu.SMEM)
NT = (((1,), (1,)), ((), ()))
NN = (((1,), (0,)), ((), ()))


def mm(a, b, dims=NN):
    return lax.dot_general(a, b, dims, preferred_element_type=f32)


def split3(x):
    hi = x.astype(bf16)
    rest = x - hi.astype(f32)
    mid = rest.astype(bf16)
    lo = (rest - mid.astype(f32)).astype(bf16)
    return hi, mid, lo


def params(mib):
    return pltpu.CompilerParams(vmem_limit_bytes=mib << 20)


def cost(us, flops=0):
    return pl.CostEstimate(flops=flops, bytes_accessed=int(us * 3_000_000), transcendentals=0)


def pack_kernel(width, half_ref, a_ref, b_ref, out_ref):
    for h in range(KVH):
        at = (h // 2) * 2 + (h % 2 + half_ref[0] - 2 * (h % 2) * half_ref[0])
        out_ref[at, :, :width] = a_ref[:, h * width : (h + 1) * width]
        out_ref[at, :, width:] = b_ref[:, h * width : (h + 1) * width]


def pack_heads(half, a, b, name):
    width = a.shape[1] // KVH
    return pl.pallas_call(
        functools.partial(pack_kernel, width),
        out_shape=jax.ShapeDtypeStruct((KVH, TOK, 2 * width), bf16),
        in_specs=[SM, VM, VM],
        out_specs=VM,
        compiler_params=params(60),
        cost_estimate=cost(2),
        name=name,
    )(half, a, b)


def mixed_kernel(
    sc_ref, owner_ref, embed_ref, scale_ref, wk_ref, wv_ref, mark_ref, u0, u1, u2, u3, wk_s, wv_s, sems
):
    at = pl.ds(pl.multiple_of(sc_ref[5] * FS, FS), FS)
    copies = (
        pltpu.make_async_copy(wk_ref.at[at], wk_s, sems.at[0]),
        pltpu.make_async_copy(wv_ref.at[at], wv_s, sems.at[1]),
    )
    for copy in copies:
        copy.start()
    mark_ref[...] = jnp.zeros_like(mark_ref)
    lane = lax.broadcasted_iota(jnp.int32, (SLOTS, 128), 1)
    scale = scale_ref[...].reshape(1, FS)
    outs = (u0, u1, u2, u3)
    scaled = []
    for n in range(NDP):
        rows = embed_ref[owner_ref[n]].astype(f32)
        tail = jnp.zeros((SLOTS, 128), f32)
        for k, part in enumerate(split3(jnp.sum(rows * rows, 1, keepdims=True))):
            tail = jnp.where(lane == k, part.astype(f32), tail)
        outs[n][:, 2 * KVH * HD :] = tail.astype(bf16)
        scaled.append((rows * scale).astype(bf16))
    scaled = jnp.concatenate(scaled, 0)
    for half, (copy, w_s) in enumerate(zip(copies, (wk_s, wv_s))):
        copy.wait()
        mixed = mm(scaled, w_s[...]).astype(bf16)
        for n in range(NDP):
            outs[n][:, half * KVH * HD : (half + 1) * KVH * HD] = mixed[
                n * SLOTS : (n + 1) * SLOTS
            ]


def mix(sc, owner, embed, scale, wk, wv):
    one = jax.ShapeDtypeStruct((SLOTS, 2 * KVH * HD + 128), bf16)
    return pl.pallas_call(
        mixed_kernel,
        out_shape=(jax.ShapeDtypeStruct((8, 128), f32),) + (one,) * NDP,
        in_specs=[SM, SM, VM, VM, ANY, ANY],
        out_specs=(VM,) * (NDP + 1),
        scratch_shapes=[
            pltpu.VMEM((FS, KVH * HD), bf16),
            pltpu.VMEM((FS, KVH * HD), bf16),
            pltpu.SemaphoreType.DMA((2,)),
        ],
        compiler_params=params(60),
        cost_estimate=cost(5),
        name="mix",
    )(sc, owner, embed, scale, wk, wv)


def join(x, *after):
    return pl.pallas_call(
        lambda *refs: None,
        out_shape=jax.ShapeDtypeStruct(x.shape, x.dtype),
        in_specs=[ANY] * (1 + len(after)),
        out_specs=ANY,
        input_output_aliases={0: 0},
        compiler_params=params(2),
        cost_estimate=cost(1),
        name="join",
    )(x, *after)


def attention_kernel(
    sc_ref,
    qd_ref,
    kv0_ref,
    kv1_ref,
    kv2_ref,
    kv3_ref,
    dq_ref,
    own_ref,
    core_ref,
    far_ref,
    farcore_ref,
    tok_ref,
    k_s,
    v_s,
    kt_s,
    q_s,
    do_s,
    e_s,
    w_s,
    p_s,
    dk_s,
    dv_s,
    tot,
    mom,
    dqt,
    perm,
    dot_s,
):
    prefix, zh, core = sc_ref[0], sc_ref[1], sc_ref[2]
    eye = (
        lax.broadcasted_iota(jnp.int32, (HD, HD), 0) == lax.broadcasted_iota(jnp.int32, (HD, HD), 1)
    ).astype(bf16)
    for seg in range(NSEG):
        near, away = ((kv0_ref, kv1_ref), (kv2_ref, kv3_ref))[seg // 4]
        y = seg % 4
        whole = jnp.concatenate([near[2 * y], near[2 * y + 1], away[2 * y], away[2 * y + 1]], 0)
        k_s[seg] = whole[:, :HD]
        v_s[seg] = whole[:, HD:]
        kt_s[seg] = mm(eye, whole[:, :HD], NT).astype(bf16)
    dk_s[...] = jnp.zeros_like(dk_s)
    dv_s[...] = jnp.zeros_like(dv_s)

    def key_start(j):
        far = j // 4
        return (j % 4) * 1024 + (zh + far - 2 * zh * far) * SEG

    def hidden(key0, row0):
        s = lax.broadcasted_iota(jnp.int32, (SEG, SEG), 0)
        piece = s // TOK
        other = piece // 2
        key = key0 + (piece % 2) * 256 + (core + other - 2 * core * other) * TOK + s % TOK
        lane = lax.broadcasted_iota(jnp.int32, (1, SEG), 1)
        row = row0 + ((lane // TOK) % 2) * 256 + lane % TOK
        return key >= jnp.maximum(row + 1, prefix)

    def row_body(i, _):
        row0 = i * 1024 + zh * SEG + core * TOK
        limit = jnp.maximum(prefix, row0 + 384)
        full = jnp.maximum(prefix, row0 + 1)
        for head in range(2):
            for z in range(2):
                at = pl.ds((head * 2 + z) * TOK, TOK)
                q_s[at, :] = qd_ref[2 * i + z, :, head * HD : (head + 1) * HD]
                do_s[at, :] = qd_ref[2 * i + z, :, (2 + head) * HD : (3 + head) * HD]
        tot[...] = jnp.zeros_like(tot)
        mom[...] = jnp.zeros_like(mom)
        dqt[...] = jnp.zeros_like(dqt)

        def scores(y, masked):
            pair = (y, y + 4)
            for j in pair:
                for c in range(0, SEG, 256):
                    cc = slice(c, c + 256)
                    t = jnp.tanh(mm(k_s[j], q_s[cc, :], NT) * tanh_scale)
                    dp = mm(v_s[j], do_s[cc, :], NT)
                    e = jnp.exp2(t * exp2_scale)
                    if masked:
                        e = jnp.where(hidden(key_start(j), row0)[:, cc], 0.0, e)
                    tot[:, cc] += jnp.sum(e, 0, keepdims=True)
                    mom[:, cc] += jnp.sum(e * dp, 0, keepdims=True)
                    e_s[j, :, cc] = e.astype(bf16)
                    w_s[j, :, cc] = e * (1.0 - t * t)
                    p_s[j, :, cc] = dp

        def first(y, _):
            @pl.when(y * 1024 + 1024 <= full)
            def _():
                scores(y, False)

            @pl.when((y * 1024 + 1024 > full) & (y * 1024 < limit))
            def _():
                scores(y, True)

            return 0

        lax.fori_loop(0, 4, first, 0)
        inv = 1.0 / tot[...]
        delta = mom[...] * inv
        dot_s[...] = (mm(eye, do_s[...], NT) * inv).astype(bf16)

        def second(y, _):
            @pl.when(y * 1024 < limit)
            def _():
                grad = dqt[...]
                for j in (y, y + 4):
                    ds = (w_s[j] * inv * (p_s[j] - delta)).astype(bf16)
                    dv_s[j] += mm(e_s[j], dot_s[...], NT)
                    dk_s[j] += mm(ds, q_s[...])
                    grad += mm(kt_s[j], ds)
                dqt[...] = grad

            return 0

        lax.fori_loop(0, 4, second, 0)
        dq = (dqt[...] * score_scale).T.astype(bf16)
        for head in range(2):
            for z in range(2):
                at = (head * 2 + z) * TOK
                dq_ref[2 * i + z, :, head * HD : (head + 1) * HD] = dq[at : at + TOK]
        return 0

    lax.fori_loop(0, 4, row_body, 0)

    out = lax.broadcasted_iota(jnp.int32, (SEG, SEG), 0)
    src = lax.broadcasted_iota(jnp.int32, (SEG, SEG), 1)
    slot = out % 16
    c_of = (slot // 4) % 2
    want = (
        (c_of + core - 2 * c_of * core) * 256 + (slot // 8) * TOK + (slot % 4) * 32 + out // 16
    )
    perm[...] = (want == src).astype(bf16)
    for seg in range(NSEG):
        near, away = ((own_ref, core_ref), (far_ref, farcore_ref))[seg // 4]
        y = seg % 4
        terms = jnp.concatenate([dk_s[seg] * score_scale, dv_s[seg]], 1)
        near[2 * y] = terms[:TOK].astype(near.dtype)
        near[2 * y + 1] = terms[TOK : 2 * TOK].astype(near.dtype)
        away[2 * y] = terms[2 * TOK : 3 * TOK].astype(away.dtype)
        away[2 * y + 1] = terms[3 * TOK :].astype(away.dtype)
        if y < 2:
            moved = mm(perm[...], terms.astype(bf16)).astype(bf16).reshape(32, 16, 2 * HD)
            z_at = zh if seg < 4 else 1 - zh
            tok_ref[:, pl.ds(pl.multiple_of((2 * y + z_at) * 16, 16), 16), :] = moved


def attention(sc, qd, kv0, kv1, kv2, kv3):
    part = (KVH, TOK, 2 * HD)
    return pl.pallas_call(
        attention_kernel,
        out_shape=(
            jax.ShapeDtypeStruct(part, bf16),
            jax.ShapeDtypeStruct(part, f32),
            jax.ShapeDtypeStruct(part, bf16),
            jax.ShapeDtypeStruct(part, bf16),
            jax.ShapeDtypeStruct(part, bf16),
            jax.ShapeDtypeStruct((32, SLOTS, 2 * HD), bf16),
        ),
        in_specs=[SM] + [VM] * 5,
        out_specs=(VM,) * 6,
        scratch_shapes=[
            pltpu.VMEM((NSEG, SEG, HD), bf16),
            pltpu.VMEM((NSEG, SEG, HD), bf16),
            pltpu.VMEM((NSEG, HD, SEG), bf16),
            pltpu.VMEM((SEG, HD), bf16),
            pltpu.VMEM((SEG, HD), bf16),
            pltpu.VMEM((NSEG, SEG, SEG), bf16),
            pltpu.VMEM((NSEG, SEG, SEG), f32),
            pltpu.VMEM((NSEG, SEG, SEG), f32),
            pltpu.VMEM((NSEG, SEG, HD), f32),
            pltpu.VMEM((NSEG, SEG, HD), f32),
            pltpu.VMEM((1, SEG), f32),
            pltpu.VMEM((1, SEG), f32),
            pltpu.VMEM((HD, SEG), f32),
            pltpu.VMEM((SEG, SEG), bf16),
            pltpu.VMEM((HD, SEG), bf16),
        ],
        compiler_params=params(60),
        cost_estimate=cost(36),
        name="attention",
    )(sc, qd, kv0, kv1, kv2, kv3)


def pair_sum_kernel(a_ref, b_ref, out_ref):
    out_ref[...] = (a_ref[...].astype(f32) + b_ref[...].astype(f32)).astype(bf16)


def pair_sum(a, b):
    return pl.pallas_call(
        pair_sum_kernel,
        out_shape=jax.ShapeDtypeStruct(a.shape, bf16),
        in_specs=[VM, VM],
        out_specs=VM,
        compiler_params=params(60),
        cost_estimate=cost(2, 3_000_000_000),
        name="pair_sum",
    )(a, b)


def last_sum_kernel(dq_ref, a_ref, b_ref, c_ref, _, out_ref):
    out_ref[:, :, : 2 * HD] = dq_ref[...]
    total = a_ref[...] + b_ref[...].astype(f32) + c_ref[...].astype(f32)
    out_ref[:, :, 2 * HD :] = total.astype(bf16)


def last_sum(dq, a, b, c, after):
    return pl.pallas_call(
        last_sum_kernel,
        out_shape=jax.ShapeDtypeStruct((KVH, TOK, 4 * HD), bf16),
        in_specs=[VM] * 4 + [ANY],
        out_specs=VM,
        compiler_params=params(8),
        cost_estimate=cost(3),
        name="last_sum",
    )(dq, a, b, c, after)


def unpack_kernel(half_ref, in_ref, q_ref, k_ref, v_ref):
    for h in range(KVH):
        at = (h // 2) * 2 + (h % 2 + half_ref[0] - 2 * (h % 2) * half_ref[0])
        q_ref[:, h * 2 * HD : (h + 1) * 2 * HD] = in_ref[at, :, : 2 * HD]
        k_ref[:, h * HD : (h + 1) * HD] = in_ref[at, :, 2 * HD : 3 * HD]
        v_ref[:, h * HD : (h + 1) * HD] = in_ref[at, :, 3 * HD :]


def unpack(half, grads):
    return pl.pallas_call(
        unpack_kernel,
        out_shape=(
            jax.ShapeDtypeStruct((TOK, 2 * KVH * HD), bf16),
            jax.ShapeDtypeStruct((TOK, KVH * HD), bf16),
            jax.ShapeDtypeStruct((TOK, KVH * HD), bf16),
        ),
        in_specs=[SM, VM],
        out_specs=(VM, VM, VM),
        compiler_params=params(8),
        cost_estimate=cost(2),
        name="unpack",
    )(half, grads)


def token_kernel(sc_ref, tok_ref, u0, u1, u2, u3, out_ref):
    token = lax.broadcasted_iota(jnp.int32, (SLOTS, 2 * HD), 0) * 32 + sc_ref[4]
    visible = token < sc_ref[3]
    wide = KVH * HD
    cross = jnp.zeros((SLOTS, 1), f32)
    for h in range(KVH):
        base = (h // 2) * 8 + (h % 2) * 2
        away = (h // 2) * 8 + 4 + (1 - h % 2) * 2
        total = tok_ref[base].astype(f32) + tok_ref[base + 1].astype(f32)
        total = total + tok_ref[away].astype(f32) + tok_ref[away + 1].astype(f32)
        total = jnp.where(visible, total, 0.0).astype(bf16)
        for half in range(2):
            at = slice(half * wide + h * HD, half * wide + (h + 1) * HD)
            part = total[:, half * HD : (half + 1) * HD]
            out_ref[:, at] = part
            mixed = u0[:, at].astype(f32) + u1[:, at].astype(f32)
            mixed = mixed + u2[:, at].astype(f32) + u3[:, at].astype(f32)
            cross += jnp.sum(part.astype(f32) * mixed, 1, keepdims=True)
    lane = lax.broadcasted_iota(jnp.int32, (SLOTS, 128), 1)
    tail = u0[:, 2 * wide :].astype(f32) + u1[:, 2 * wide :].astype(f32)
    tail = tail + u2[:, 2 * wide :].astype(f32) + u3[:, 2 * wide :].astype(f32)
    sq = jnp.sum(tail, 1, keepdims=True)
    parts = split3(lax.rsqrt(sq / D + norm_eps)) + split3(cross / D)
    tail = jnp.zeros((SLOTS, 128), f32)
    for n, part in enumerate(parts):
        tail = jnp.where(lane == n, part.astype(f32), tail)
    out_ref[:, 2 * wide :] = tail.astype(bf16)


def token_rows(sc, tok, mixed):
    return pl.pallas_call(
        token_kernel,
        out_shape=jax.ShapeDtypeStruct((SLOTS, 2 * KVH * HD + 128), bf16),
        in_specs=[SM] + [VM] * 5,
        out_specs=VM,
        compiler_params=params(60),
        cost_estimate=cost(2),
        name="token_rows",
    )(sc, tok, *mixed)


def image_kernel(
    sc_ref, owner_ref, r0, r1, r2, r3, wk_ref, wv_ref, embed_ref, scale_ref, out_ref, wk_s, wv_s, sems
):
    at = pl.ds(pl.multiple_of(sc_ref[5] * FS, FS), FS)
    copies = (
        pltpu.make_async_copy(wk_ref.at[at], wk_s, sems.at[0]),
        pltpu.make_async_copy(wv_ref.at[at], wv_s, sems.at[1]),
    )
    for copy in copies:
        copy.start()
    wide = KVH * HD
    recvs = (r0, r1, r2, r3)
    xk = jnp.concatenate([r[:, :wide] for r in recvs], 0)
    xv = jnp.concatenate([r[:, wide : 2 * wide] for r in recvs], 0)
    copies[0].wait()
    projected = mm(xk, wk_s[...], NT)
    copies[1].wait()
    projected = projected + mm(xv, wv_s[...], NT)
    lane = lax.broadcasted_iota(jnp.int32, (SLOTS, 128), 1)
    scale = scale_ref[...].reshape(1, FS)
    for n, recv_ref in enumerate(recvs):
        row = owner_ref[n]
        tail = recv_ref[:, 2 * wide :].astype(f32)
        inv = jnp.sum(jnp.where(lane < 3, tail, 0.0), 1, keepdims=True)
        cross = jnp.sum(jnp.where(lane >= 3, tail, 0.0), 1, keepdims=True)
        grad = projected[n * SLOTS : (n + 1) * SLOTS].astype(bf16).astype(f32)
        rows = embed_ref[row].astype(f32)
        out_ref[row] = inv * (scale * grad) - rows * (inv * inv * inv * cross)


def image_out(sc, owner, recvs, wk, wv, embed, scale):
    return pl.pallas_call(
        image_kernel,
        out_shape=jax.ShapeDtypeStruct((NDP, SLOTS, FS), f32),
        in_specs=[SM, SM] + [VM] * 4 + [ANY, ANY, VM, VM],
        out_specs=VM,
        scratch_shapes=[
            pltpu.VMEM((FS, KVH * HD), bf16),
            pltpu.VMEM((FS, KVH * HD), bf16),
            pltpu.SemaphoreType.DMA((2,)),
        ],
        compiler_params=params(60),
        cost_estimate=cost(5, 60_000_000_000),
        name="image_out",
    )(sc, owner, *recvs, wk, wv, embed, scale)


def exchange(x, axes):
    return lax.all_to_all(x, axes, split_axis=0, concat_axis=0, tiled=True)


def shift(x, by):
    return lax.ppermute(x, "dp", [(i, (i + by) % NDP) for i in range(NDP)])


def mirror(x):
    return lax.ppermute(x, ("zh", "zl"), [(i, 3 - i) for i in range(4)])


def swap(x, axis):
    return lax.ppermute(x, axis, [(0, 1), (1, 0)])


def local(
    query_states,
    key_states,
    value_states,
    out_grads,
    image_counts,
    prefix_lengths,
    encoder_owner,
    key_weight,
    value_weight,
    norm_scale,
    image_embed,
):
    ctx = ("y", "zh", "zl", "core")
    dp = lax.axis_index("dp")
    half = lax.axis_index("zh").astype(jnp.int32).reshape(1)
    sc = jnp.stack(
        [
            prefix_lengths[0],
            lax.axis_index("zh"),
            lax.axis_index("core"),
            image_counts[0],
            lax.axis_index(ctx),
            dp,
        ]
    ).astype(jnp.int32)
    owner = lax.dynamic_slice(jnp.concatenate([encoder_owner, encoder_owner]), (dp,), (NDP,))

    kv0 = exchange(pack_heads(half, key_states[0], value_states[0], "pack_kv"), ("y", "zl"))
    qd_pack = pack_heads(half, query_states[0], out_grads[0], "pack_qd")
    mark, *mixed = mix(sc, owner, image_embed, norm_scale, key_weight, value_weight)
    kv0 = join(kv0, mark, qd_pack)
    kv1 = swap(kv0, "core")
    mixed = [mixed[0]] + [shift(mixed[n], n) for n in range(1, NDP)]
    kv2 = join(mirror(kv0), mixed[1], mixed[3])
    kv3 = swap(kv2, "core")
    qd = exchange(qd_pack, ("y", "zl"))

    dq, own, core_part, far, farcore, tok = attention(sc, qd, kv0, kv1, kv2, kv3)

    tok_in = exchange(tok, ctx)
    far_sum = pair_sum(far, swap(farcore, "core"))
    rows = token_rows(sc, tok_in, mixed)
    grads = last_sum(dq, own, swap(core_part, "core"), mirror(far_sum), rows)
    recvs = [rows] + [shift(rows, -n) for n in range(1, NDP)]
    image_grads = image_out(
        sc, owner, recvs, key_weight, value_weight, image_embed, norm_scale
    )
    query_grads, key_grads, value_grads = unpack(half, exchange(grads, ("y", "zl")))
    return (query_grads[None], key_grads[None], value_grads[None], image_grads)


def solution(mesh):
    ctx = ("y", "zh", "zl", "core")
    split = Mesh(mesh.devices.reshape(4, 4, 2, 2, 2), ("dp",) + ctx)
    rows = P("dp", ctx, None)
    image = P(None, ctx, "dp")
    in_specs = (rows, rows, rows, rows, P("dp"), P("dp"), P(), P(), P(), P("dp"), image)
    out_specs = (rows, rows, rows, image)
    return jax.shard_map(local, mesh=split, in_specs=in_specs, out_specs=out_specs, check_vma=False)
```

profile of v0, /device:TPU:0, one launch (start us, length us, event | category | flops | bytes accessed | tf_op | source)
XLA Modules:
  0.0 130.5 jit_solution(14418990224256301028)
XLA Ops:
  0.6 1.9 %pack_kv.1 = bf16[8,128,256]{2,1,0:T(8,128)(2,1)} custom-call(s32[1]{0:T(128)} %bitcast.half_ref, bf16[128,1024]{1,0:T(8,128)(2,1)} %bitcast.13, bf16[128,1024]{1,0:T(8,128)(2,1)} %bitcast.14), custom_call_target="tpu_custom_call" | custom-call | bytes 6000000 | tf_op jit(solution)/shard_map/pack_kv/pallas_call | solution.py:65
  2.6 5.9 %all-to-all-start.1 = ((bf16[8,128,256]{2,1,0:T(8,128)(2,1)}), bf16[8,128,256]{2,1,0:T(8,128)(2,1)S(1)}, u32[]{:S(2)}, u32[]{:S(2)}) async-start(bf16[8,128,256]{2,1,0:T(8,128)(2,1)} %pack_kv.1), calls=%async_computation.1 | async-start | bytes 1048576 | tf_op jit(solution)/shard_map/all_to_all | solution.py:469
  11.2 2.3 %pack_qd.1.refs_2_ = bf16[8,128,512]{2,1,0:T(8,128)(2,1)} custom-call(s32[1]{0:T(128)} %bitcast.half_ref, bf16[128,2048]{1,0:T(8,128)(2,1)} %bitcast.11, bf16[128,2048]{1,0:T(8,128)(2,1)} %bitcast.12), custom_call_target="tpu_custom_call" | custom-call | bytes 6000000 | tf_op jit(solution)/shard_map/pack_qd/pallas_call | solution.py:65
  14.1 5.4 %mix.1 = (f32[8,128]{1,0:T(8,128)}, bf16[64,2176]{1,0:T(8,128)(2,1)}, bf16[64,2176]{1,0:T(8,128)(2,1)}, bf16[64,2176]{1,0:T(8,128)(2,1)}, bf16[64,2176]{1,0:T(8,128)(2,1)}) custom-call(s32[6]{0:T(128)} %stack.16.sc_ref, s32[4]{0:T(128)} %dynamic_slice.3.owner_ref, bf16[4,64,1152]{2,1,0:T(8,128)(2,1)} %embed_ref.3, f32[1152]{0:T(1024)} %scale_ref.3, ...), custom_call_target="tpu_custom_call" | custom-call | bytes 15000000 | tf_op jit(solution)/shard_map/mix/pallas_call | solution.py:110
  20.2 4.1 %collective-permute-start.1 = (bf16[8,128,256]{2,1,0:T(8,128)(2,1)S(1)}, bf16[8,128,256]{2,1,0:T(8,128)(2,1)S(1)}, u32[]{:S(2)}, u32[]{:S(2)}) collective-permute-start(bf16[8,128,256]{2,1,0:T(8,128)(2,1)S(1)} %join.2.kv0_ref), channel_id=1, source_target_pairs={{0,6},{2,4},{4,2},{6,0},{1,7},{3,5},{5,3},{7,1},{8,14},{10,12},{12... | collective-permute-start | bytes 1572872 | tf_op jit(solution)/shard_map/ppermute | solution.py:477
  24.3 4.2 %all-to-all-start = ((bf16[8,128,512]{2,1,0:T(8,128)(2,1)}), bf16[8,128,512]{2,1,0:T(8,128)(2,1)S(1)}, u32[]{:S(2)}, u32[]{:S(2)}) async-start(bf16[8,128,512]{2,1,0:T(8,128)(2,1)} %pack_qd.1.refs_2_), calls=%async_computation | async-start | bytes 2097152 | tf_op jit(solution)/shard_map/all_to_all | solution.py:469
  28.6 1.5 %collective-permute-start.2 = (bf16[64,2176]{1,0:T(8,128)(2,1)}, bf16[64,2176]{1,0:T(8,128)(2,1)S(1)}, u32[]{:S(2)}, u32[]{:S(2)}) collective-permute-start(bf16[64,2176]{1,0:T(8,128)(2,1)} %get-tuple-element.19), channel_id=1, source_target_pairs={{0,32},{32,64},{64,96},{96,0},{1,33},{33,65},{65,97},{97,1},{2,34}... | collective-permute-start | bytes 835592 | tf_op jit(solution)/shard_map/ppermute | solution.py:473
  30.1 1.7 %collective-permute-start.3 = (bf16[64,2176]{1,0:T(8,128)(2,1)}, bf16[64,2176]{1,0:T(8,128)(2,1)S(1)}, u32[]{:S(2)}, u32[]{:S(2)}) collective-permute-start(bf16[64,2176]{1,0:T(8,128)(2,1)} %get-tuple-element.20), channel_id=1, source_target_pairs={{0,96},{32,0},{64,32},{96,64},{1,97},{33,1},{65,33},{97,65},{2,98}... | collective-permute-start | bytes 835592 | tf_op jit(solution)/shard_map/ppermute | solution.py:473
  31.8 5.5 %collective-permute-done.2.refs_1_.u1 = bf16[64,2176]{1,0:T(8,128)(2,1)S(1)} collective-permute-done((bf16[64,2176]{1,0:T(8,128)(2,1)}, bf16[64,2176]{1,0:T(8,128)(2,1)S(1)}, u32[]{:S(2)}, u32[]{:S(2)}) %collective-permute-start.2) | collective-permute-done | bytes 278560 | tf_op jit(solution)/shard_map/ppermute | solution.py:473
  37.4 5.9 %all-to-all-done.qd_ref = bf16[8,128,512]{2,1,0:T(8,128)(2,1)S(1)} async-done(((bf16[8,128,512]{2,1,0:T(8,128)(2,1)}), bf16[8,128,512]{2,1,0:T(8,128)(2,1)S(1)}, u32[]{:S(2)}, u32[]{:S(2)}) %all-to-all-start) | async-done | bytes 1048608 | tf_op jit(solution)/shard_map/all_to_all | solution.py:469
  44.5 31.0 %attention.1 = (bf16[8,128,256]{2,1,0:T(8,128)(2,1)}, f32[8,128,256]{2,1,0:T(8,128)}, bf16[8,128,256]{2,1,0:T(8,128)(2,1)}, bf16[8,128,256]{2,1,0:T(8,128)(2,1)}...) custom-call(s32[6]{0:T(128)} %stack.16.sc_ref, bf16[8,128,512]{2,1,0:T(8,128)(2,1)} %copy-done.8, ...), custom_call_target="tpu_custom_call" | custom-call | bytes 108000000 | tf_op jit(solution)/shard_map/attention/pallas_call | solution.py:287
  75.6 4.8 %all-to-all-start.2 = ((bf16[32,64,256]{2,1,0:T(8,128)(2,1)}), bf16[32,64,256]{2,1,0:T(8,128)(2,1)}, u32[]{:S(2)}, u32[]{:S(2)}) async-start(bf16[32,64,256]{2,1,0:T(8,128)(2,1)} %get-tuple-element.26), calls=%async_computation.2 | async-start | bytes 2097152 | tf_op jit(solution)/shard_map/all_to_all | solution.py:469
  81.5 2.1 %pair_sum.1 = bf16[8,128,256]{2,1,0:T(8,128)(2,1)} custom-call(bf16[8,128,256]{2,1,0:T(8,128)(2,1)} %get-tuple-element.24.a_ref, bf16[8,128,256]{2,1,0:T(8,128)(2,1)} %copy-done.11), custom_call_target="tpu_custom_call" | custom-call | flops 3000000000 | bytes 6000000 | tf_op jit(solution)/shard_map/pair_sum/pallas_call | solution.py:327
  83.6 2.9 %collective-permute-start.7 = (bf16[8,128,256]{2,1,0:T(8,128)(2,1)}, bf16[8,128,256]{2,1,0:T(8,128)(2,1)S(1)}, u32[]{:S(2)}, u32[]{:S(2)}) collective-permute-start(bf16[8,128,256]{2,1,0:T(8,128)(2,1)} %pair_sum.1), channel_id=1, source_target_pairs={{0,6},{2,4},{4,2},{6,0},{1,7},{3,5},{5,3},{7,1},{8,14},{10,12},{12... | collective-permute-start | bytes 1572872 | tf_op jit(solution)/shard_map/ppermute | solution.py:477
  86.5 4.4 %collective-permute-done.8.u2 = bf16[64,2176]{1,0:T(8,128)(2,1)S(1)} collective-permute-done((bf16[64,2176]{1,0:T(8,128)(2,1)}, bf16[64,2176]{1,0:T(8,128)(2,1)S(1)}, u32[]{:S(2)}, u32[]{:S(2)}) %collective-permute-start.8) | collective-permute-done | bytes 278560 | tf_op jit(solution)/shard_map/ppermute | solution.py:473
  90.9 6.3 %all-to-all-done.2.tok_ref = bf16[32,64,256]{2,1,0:T(8,128)(2,1)} async-done(((bf16[32,64,256]{2,1,0:T(8,128)(2,1)}), bf16[32,64,256]{2,1,0:T(8,128)(2,1)}, u32[]{:S(2)}, u32[]{:S(2)}) %all-to-all-start.2) | async-done | bytes 1048608 | tf_op jit(solution)/shard_map/all_to_all | solution.py:469
  97.2 2.7 %token_rows.1._.r0 = bf16[64,2176]{1,0:T(8,128)(2,1)} custom-call(s32[6]{0:T(128)} %stack.16.sc_ref, bf16[32,64,256]{2,1,0:T(8,128)(2,1)} %all-to-all-done.2.tok_ref, bf16[64,2176]{1,0:T(8,128)(2,1)} %get-tuple-element.27.u0, bf16[64,2176]{1,0:T(8,128)(2,1)} %copy-done.2, bf16[64,2176]{1,0:T(8,128)(2,1)} %copy-done.10, bf16[64,2176]{1,0:T(8,128)(2,1)} %copy-done.3), custom_call_target="tpu_custom_call" | custom-call | bytes 6000000 | tf_op jit(solution)/shard_map/token_rows/pallas_call | solution.py:410
  100.6 2.7 %collective-permute-start.9 = (bf16[64,2176]{1,0:T(8,128)(2,1)}, bf16[64,2176]{1,0:T(8,128)(2,1)}, u32[]{:S(2)}, u32[]{:S(2)}) collective-permute-start(bf16[64,2176]{1,0:T(8,128)(2,1)} %token_rows.1._.r0), channel_id=1, source_target_pairs={{0,96},{32,0},{64,32},{96,64},{1,97},{33,1},{65,33},{97,65},{2,98}... | collective-permute-start | bytes 835592 | tf_op jit(solution)/shard_map/ppermute | solution.py:473
  103.3 3.4 %collective-permute-done.7.c_ref = bf16[8,128,256]{2,1,0:T(8,128)(2,1)S(1)} collective-permute-done((bf16[8,128,256]{2,1,0:T(8,128)(2,1)}, bf16[8,128,256]{2,1,0:T(8,128)(2,1)S(1)}, u32[]{:S(2)}, u32[]{:S(2)}) %collective-permute-start.7) | collective-permute-done | bytes 524320 | tf_op jit(solution)/shard_map/ppermute | solution.py:477
  107.7 1.2 last_sum.1
  108.9 4.4 %all-to-all-start.3 = ((bf16[8,128,512]{2,1,0:T(8,128)(2,1)}), bf16[8,128,512]{2,1,0:T(8,128)(2,1)S(1)}, u32[]{:S(2)}, u32[]{:S(2)}) async-start(bf16[8,128,512]{2,1,0:T(8,128)(2,1)} %last_sum.1), calls=%async_computation.3 | async-start | bytes 2097152 | tf_op jit(solution)/shard_map/all_to_all | solution.py:469
  113.3 2.9 %collective-permute-done.11.r3 = bf16[64,2176]{1,0:T(8,128)(2,1)S(1)} collective-permute-done((bf16[64,2176]{1,0:T(8,128)(2,1)}, bf16[64,2176]{1,0:T(8,128)(2,1)S(1)}, u32[]{:S(2)}, u32[]{:S(2)}) %collective-permute-start.11) | collective-permute-done | bytes 278560 | tf_op jit(solution)/shard_map/ppermute | solution.py:473
  116.9 6.5 %image_out.1 = f32[4,64,1152]{2,1,0:T(8,128)} custom-call(s32[6]{0:T(128)} %stack.16.sc_ref, s32[4]{0:T(128)} %dynamic_slice.3.owner_ref, bf16[64,2176]{1,0:T(8,128)(2,1)} %token_rows.1._.r0, bf16[64,2176]{1,0:T(8,128)(2,1)} %collective-permute-done.9.r1, bf16[64,2176]{1,0:T(8,128)(2,1)} %collective-permute-done.10.r2, bf16[64,2176]{1,0:T(8,128)(2,1)} %copy-done.12, ...), custom_call_target="tpu_custom_call" | custom-call | flops 60000002048 | bytes 15000000 | tf_op jit(solution)/shard_map/image_out/pallas_call | solution.py:452
  123.4 6.0 %all-to-all-done.3.in_ref = bf16[8,128,512]{2,1,0:T(8,128)(2,1)S(1)} async-done(((bf16[8,128,512]{2,1,0:T(8,128)(2,1)}), bf16[8,128,512]{2,1,0:T(8,128)(2,1)S(1)}, u32[]{:S(2)}, u32[]{:S(2)}) %all-to-all-start.3) | async-done | bytes 1048608 | tf_op jit(solution)/shard_map/all_to_all | solution.py:469
  (48 shorter events, 8.8 us)
Async XLA Ops:
  2.6 16.9 %all-to-all-start.1 = ((bf16[8,128,256]{2,1,0:T(8,128)(2,1)}), bf16[8,128,256]{2,1,0:T(8,128)(2,1)S(1)}, u32[]{:S(2)}, u32[]{:S(2)}) async-start(bf16[8,128,256]{2,1,0:T(8,128)(2,1)} %pack_kv.1), calls=%async_computation.1 | async-start | bytes 1048576 | tf_op jit(solution)/shard_map/all_to_all | solution.py:469
  20.2 23.1 %copy-start = (bf16[8,128,256]{2,1,0:T(8,128)(2,1)}, bf16[8,128,256]{2,1,0:T(8,128)(2,1)S(1)}, u32[]{:S(2)}) copy-start(bf16[8,128,256]{2,1,0:T(8,128)(2,1)S(1)} %join.2.kv0_ref) | copy-start | bytes 1572868
  20.2 17.1 %collective-permute-start.1 = (bf16[8,128,256]{2,1,0:T(8,128)(2,1)S(1)}, bf16[8,128,256]{2,1,0:T(8,128)(2,1)S(1)}, u32[]{:S(2)}, u32[]{:S(2)}) collective-permute-start(bf16[8,128,256]{2,1,0:T(8,128)(2,1)S(1)} %join.2.kv0_ref), channel_id=1, source_target_pairs={{0,6},{2,4},{4,2},{6,0},{1,7},{3,5},{5,3},{7,1},{8,14},{10,12},{12... | collective-permute-start | bytes 1572872 | tf_op jit(solution)/shard_map/ppermute | solution.py:477
  24.3 19.0 %all-to-all-start = ((bf16[8,128,512]{2,1,0:T(8,128)(2,1)}), bf16[8,128,512]{2,1,0:T(8,128)(2,1)S(1)}, u32[]{:S(2)}, u32[]{:S(2)}) async-start(bf16[8,128,512]{2,1,0:T(8,128)(2,1)} %pack_qd.1.refs_2_), calls=%async_computation | async-start | bytes 2097152 | tf_op jit(solution)/shard_map/all_to_all | solution.py:469
  28.6 8.7 %collective-permute-start.2 = (bf16[64,2176]{1,0:T(8,128)(2,1)}, bf16[64,2176]{1,0:T(8,128)(2,1)S(1)}, u32[]{:S(2)}, u32[]{:S(2)}) collective-permute-start(bf16[64,2176]{1,0:T(8,128)(2,1)} %get-tuple-element.19), channel_id=1, source_target_pairs={{0,32},{32,64},{64,96},{96,0},{1,33},{33,65},{65,97},{97,1},{2,34}... | collective-permute-start | bytes 835592 | tf_op jit(solution)/shard_map/ppermute | solution.py:473
  30.1 7.2 %collective-permute-start.3 = (bf16[64,2176]{1,0:T(8,128)(2,1)}, bf16[64,2176]{1,0:T(8,128)(2,1)S(1)}, u32[]{:S(2)}, u32[]{:S(2)}) collective-permute-start(bf16[64,2176]{1,0:T(8,128)(2,1)} %get-tuple-element.20), channel_id=1, source_target_pairs={{0,96},{32,0},{64,32},{96,64},{1,97},{33,1},{65,33},{97,65},{2,98}... | collective-permute-start | bytes 835592 | tf_op jit(solution)/shard_map/ppermute | solution.py:473
  31.8 11.5 %collective-permute-start = (bf16[8,128,256]{2,1,0:T(8,128)(2,1)S(1)}, bf16[8,128,256]{2,1,0:T(8,128)(2,1)S(1)}, u32[]{:S(2)}, u32[]{:S(2)}) collective-permute-start(bf16[8,128,256]{2,1,0:T(8,128)(2,1)S(1)} %join.2.kv0_ref), channel_id=1, source_target_pairs={{0,1},{1,0},{2,3},{3,2},{4,5},{5,4},{6,7},{7,6},{8,9},{9,8},{10,11... | collective-permute-start | bytes 1572872 | tf_op jit(solution)/shard_map/ppermute | solution.py:481
  37.3 59.9 %copy-start.2 = (bf16[64,2176]{1,0:T(8,128)(2,1)}, bf16[64,2176]{1,0:T(8,128)(2,1)S(1)}, u32[]{:S(2)}) copy-start(bf16[64,2176]{1,0:T(8,128)(2,1)S(1)} %collective-permute-done.2.refs_1_.u1) | copy-start | bytes 835588
  37.3 59.9 %copy-start.3 = (bf16[64,2176]{1,0:T(8,128)(2,1)}, bf16[64,2176]{1,0:T(8,128)(2,1)S(1)}, u32[]{:S(2)}) copy-start(bf16[64,2176]{1,0:T(8,128)(2,1)S(1)} %collective-permute-done.3.refs_2_.u3) | copy-start | bytes 835588
  37.3 6.0 %copy-start.1 = (bf16[8,128,256]{2,1,0:T(8,128)(2,1)}, bf16[8,128,256]{2,1,0:T(8,128)(2,1)S(1)}, u32[]{:S(2)}) copy-start(bf16[8,128,256]{2,1,0:T(8,128)(2,1)S(1)} %join.3.kv2_ref) | copy-start | bytes 1572868
  37.3 6.0 %collective-permute-start.4 = (bf16[8,128,256]{2,1,0:T(8,128)(2,1)S(1)}, bf16[8,128,256]{2,1,0:T(8,128)(2,1)}, u32[]{:S(2)}, u32[]{:S(2)}) collective-permute-start(bf16[8,128,256]{2,1,0:T(8,128)(2,1)S(1)} %join.3.kv2_ref), channel_id=1, source_target_pairs={{0,1},{1,0},{2,3},{3,2},{4,5},{5,4},{6,7},{7,6},{8,9},{9,8},{10,11... | collective-permute-start | bytes 1572872 | tf_op jit(solution)/shard_map/ppermute | solution.py:481
  43.3 1.2 copy-start.9
  75.5 31.2 %copy-start.5 = (f32[8,128,256]{2,1,0:T(8,128)S(1)}, f32[8,128,256]{2,1,0:T(8,128)}, u32[]{:S(2)}) copy-start(f32[8,128,256]{2,1,0:T(8,128)} %get-tuple-element.22.a_ref) | copy-start | bytes 3145732
  75.5 31.2 %copy-start.6 = (bf16[8,128,256]{2,1,0:T(8,128)(2,1)S(1)}, bf16[8,128,256]{2,1,0:T(8,128)(2,1)}, u32[]{:S(2)}) copy-start(bf16[8,128,256]{2,1,0:T(8,128)(2,1)} %get-tuple-element.21.dq_ref) | copy-start | bytes 1572868
  75.5 5.2 %collective-permute-start.6 = (bf16[8,128,256]{2,1,0:T(8,128)(2,1)}, bf16[8,128,256]{2,1,0:T(8,128)(2,1)S(1)}, u32[]{:S(2)}, u32[]{:S(2)}) collective-permute-start(bf16[8,128,256]{2,1,0:T(8,128)(2,1)} %get-tuple-element.25), channel_id=1, source_target_pairs={{0,1},{1,0},{2,3},{3,2},{4,5},{5,4},{6,7},{7,6},{8,9},{9,8},{10,11... | collective-permute-start | bytes 1572872 | tf_op jit(solution)/shard_map/ppermute | solution.py:481
  75.6 21.6 %all-to-all-start.2 = ((bf16[32,64,256]{2,1,0:T(8,128)(2,1)}), bf16[32,64,256]{2,1,0:T(8,128)(2,1)}, u32[]{:S(2)}, u32[]{:S(2)}) async-start(bf16[32,64,256]{2,1,0:T(8,128)(2,1)} %get-tuple-element.26), calls=%async_computation.2 | async-start | bytes 2097152 | tf_op jit(solution)/shard_map/all_to_all | solution.py:469
  80.4 10.5 %collective-permute-start.8 = (bf16[64,2176]{1,0:T(8,128)(2,1)}, bf16[64,2176]{1,0:T(8,128)(2,1)S(1)}, u32[]{:S(2)}, u32[]{:S(2)}) collective-permute-start(bf16[64,2176]{1,0:T(8,128)(2,1)} %get-tuple-element.28), channel_id=1, source_target_pairs={{0,64},{32,96},{64,0},{96,32},{1,65},{33,97},{65,1},{97,33},{2,66}... | collective-permute-start | bytes 835592 | tf_op jit(solution)/shard_map/ppermute | solution.py:473
  80.5 22.8 %collective-permute-start.5 = (bf16[8,128,256]{2,1,0:T(8,128)(2,1)}, bf16[8,128,256]{2,1,0:T(8,128)(2,1)S(1)}, u32[]{:S(2)}, u32[]{:S(2)}) collective-permute-start(bf16[8,128,256]{2,1,0:T(8,128)(2,1)} %get-tuple-element.23), channel_id=1, source_target_pairs={{0,1},{1,0},{2,3},{3,2},{4,5},{5,4},{6,7},{7,6},{8,9},{9,8},{10,11... | collective-permute-start | bytes 1572872 | tf_op jit(solution)/shard_map/ppermute | solution.py:481
  83.6 23.1 %collective-permute-start.7 = (bf16[8,128,256]{2,1,0:T(8,128)(2,1)}, bf16[8,128,256]{2,1,0:T(8,128)(2,1)S(1)}, u32[]{:S(2)}, u32[]{:S(2)}) collective-permute-start(bf16[8,128,256]{2,1,0:T(8,128)(2,1)} %pair_sum.1), channel_id=1, source_target_pairs={{0,6},{2,4},{4,2},{6,0},{1,7},{3,5},{5,3},{7,1},{8,14},{10,12},{12... | collective-permute-start | bytes 1572872 | tf_op jit(solution)/shard_map/ppermute | solution.py:477
  90.9 6.3 %copy-start.10 = (bf16[64,2176]{1,0:T(8,128)(2,1)}, bf16[64,2176]{1,0:T(8,128)(2,1)S(1)}, u32[]{:S(2)}) copy-start(bf16[64,2176]{1,0:T(8,128)(2,1)S(1)} %collective-permute-done.8.u2) | copy-start | bytes 835588
  99.9 16.3 %collective-permute-start.11 = (bf16[64,2176]{1,0:T(8,128)(2,1)}, bf16[64,2176]{1,0:T(8,128)(2,1)S(1)}, u32[]{:S(2)}, u32[]{:S(2)}) collective-permute-start(bf16[64,2176]{1,0:T(8,128)(2,1)} %token_rows.1._.r0), channel_id=1, source_target_pairs={{0,32},{32,64},{64,96},{96,0},{1,33},{33,65},{65,97},{97,1},{2,34}... | collective-permute-start | bytes 835592 | tf_op jit(solution)/shard_map/ppermute | solution.py:473
  100.6 15.6 %collective-permute-start.10 = (bf16[64,2176]{1,0:T(8,128)(2,1)}, bf16[64,2176]{1,0:T(8,128)(2,1)}, u32[]{:S(2)}, u32[]{:S(2)}) collective-permute-start(bf16[64,2176]{1,0:T(8,128)(2,1)} %token_rows.1._.r0), channel_id=1, source_target_pairs={{0,64},{32,96},{64,0},{96,32},{1,65},{33,97},{65,1},{97,33},{2,66}... | collective-permute-start | bytes 835592 | tf_op jit(solution)/shard_map/ppermute | solution.py:473
  100.6 16.3 %collective-permute-start.9 = (bf16[64,2176]{1,0:T(8,128)(2,1)}, bf16[64,2176]{1,0:T(8,128)(2,1)}, u32[]{:S(2)}, u32[]{:S(2)}) collective-permute-start(bf16[64,2176]{1,0:T(8,128)(2,1)} %token_rows.1._.r0), channel_id=1, source_target_pairs={{0,96},{32,0},{64,32},{96,64},{1,97},{33,1},{65,33},{97,65},{2,98}... | collective-permute-start | bytes 835592 | tf_op jit(solution)/shard_map/ppermute | solution.py:473
  108.9 20.5 %all-to-all-start.3 = ((bf16[8,128,512]{2,1,0:T(8,128)(2,1)}), bf16[8,128,512]{2,1,0:T(8,128)(2,1)S(1)}, u32[]{:S(2)}, u32[]{:S(2)}) async-start(bf16[8,128,512]{2,1,0:T(8,128)(2,1)} %last_sum.1), calls=%async_computation.3 | async-start | bytes 2097152 | tf_op jit(solution)/shard_map/all_to_all | solution.py:469
  (5 other events, 4.1 us)
where the time goes:
time: 131 us
  Pallas kernels  54.2 us (41%)
  waiting for transfers between devices  35.1 us (27%)
  starting transfers between devices  33.5 us (26%)
  local copies, waits for them, and re-layouts  4.83 us (4%)
  between operations  2.08 us (2%)
    pallas_call x1, Pallas kernels, attention(): pl.pallas_call(attention_kernel, out_shape=(jax.ShapeDtypeStruct(part, bf...  31 us
    all_to_all x4, starting transfers between devices, exchange(): return lax.all_to_all(x, axes, split_axis=0, concat_axis=0, tiled=True)  19.4 us
    all_to_all x4, waiting for transfers between devices, exchange(): return lax.all_to_all(x, axes, split_axis=0, concat_axis=0, tiled=True)  18.1 us
    ppermute x6, waiting for transfers between devices, shift(): return lax.ppermute(x, 'dp', [(i, (i + by) % NDP) for i in range(NDP)])  13.5 us
    ppermute x2, starting transfers between devices, mirror(): return lax.ppermute(x, ('zh', 'zl'), [(i, 3 - i) for i in range(4)])  7.01 us
    ppermute x6, starting transfers between devices, shift(): return lax.ppermute(x, 'dp', [(i, (i + by) % NDP) for i in range(NDP)])  6.76 us
    pallas_call x1, Pallas kernels, image_out(): pl.pallas_call(image_kernel, out_shape=jax.ShapeDtypeStruct((NDP, SLOTS,...  6.47 us
    pallas_call x1, Pallas kernels, mix(): pl.pallas_call(mixed_kernel, out_shape=(jax.ShapeDtypeStruct((8, 128), f3...  5.41 us
  transfers between devices with their start and end apart: 16, of which 8 were waited for; matrix products, arithmetic and copies ran while one was open for 2% of the time, Pallas kernels for 15%

commit v1 on v0

--- a/solution.py
+++ b/solution.py
@@ -329,28 +329,28 @@
         out_shape=jax.ShapeDtypeStruct(a.shape, bf16),
         in_specs=[VM, VM],
         out_specs=VM,
-        compiler_params=params(60),
+        compiler_params=params(8),
         cost_estimate=cost(2, 3_000_000_000),
         name="pair_sum",
     )(a, b)
 
 
-def last_sum_kernel(dq_ref, a_ref, b_ref, c_ref, _, out_ref):
+def last_sum_kernel(dq_ref, a_ref, b_ref, c_ref, out_ref):
     out_ref[:, :, : 2 * HD] = dq_ref[...]
     total = a_ref[...] + b_ref[...].astype(f32) + c_ref[...].astype(f32)
     out_ref[:, :, 2 * HD :] = total.astype(bf16)
 
 
-def last_sum(dq, a, b, c, after):
+def last_sum(dq, a, b, c):
     return pl.pallas_call(
         last_sum_kernel,
         out_shape=jax.ShapeDtypeStruct((KVH, TOK, 4 * HD), bf16),
-        in_specs=[VM] * 4 + [ANY],
+        in_specs=[VM] * 4,
         out_specs=VM,
         compiler_params=params(8),
         cost_estimate=cost(3),
         name="last_sum",
-    )(dq, a, b, c, after)
+    )(dq, a, b, c)
 
 
 def unpack_kernel(half_ref, in_ref, q_ref, k_ref, v_ref):
@@ -524,7 +524,7 @@
     tok_in = exchange(tok, ctx)
     far_sum = pair_sum(far, swap(farcore, "core"))
     rows = token_rows(sc, tok_in, mixed)
-    grads = last_sum(dq, own, swap(core_part, "core"), mirror(far_sum), rows)
+    grads = last_sum(dq, own, swap(core_part, "core"), mirror(far_sum))
     recvs = [rows] + [shift(rows, -n) for n in range(1, NDP)]
     image_grads = image_out(
         sc, owner, recvs, key_weight, value_weight, image_embed, norm_scale

time: 131 us -> 130 us (level)
  Pallas kernels: 54.2 us -> 52.2 us
    ppermute x6, waiting for transfers between devices: 13.5 us -> 15.4 us  [shift(): return lax.ppermute(x, 'dp', [(i, (i + by) % NDP) for i in range(NDP)])]
    unnamed x26 -> x24, local copies, waits for them, and re-layouts: 3.59 us -> 2.87 us
where the time goes in v1:
time: 130 us; the launch traced here: 129 us
  Pallas kernels  52.2 us (40%)
  waiting for transfers between devices  36 us (28%)
  starting transfers between devices  33.4 us (26%)
  local copies, waits for them, and re-layouts  4.11 us (3%)
  between operations  2.07 us (2%)
    pallas_call x1, Pallas kernels, attention(): pl.pallas_call(attention_kernel, out_shape=(jax.ShapeDtypeStruct(part, bf...  30.3 us
    all_to_all x4, starting transfers between devices, exchange(): return lax.all_to_all(x, axes, split_axis=0, concat_axis=0, tiled=True)  19.4 us
    all_to_all x4, waiting for transfers between devices, exchange(): return lax.all_to_all(x, axes, split_axis=0, concat_axis=0, tiled=True)  17 us
    ppermute x6, waiting for transfers between devices, shift(): return lax.ppermute(x, 'dp', [(i, (i + by) % NDP) for i in range(NDP)])  15.4 us
    ppermute x2, starting transfers between devices, mirror(): return lax.ppermute(x, ('zh', 'zl'), [(i, 3 - i) for i in range(4)])  6.99 us
    ppermute x6, starting transfers between devices, shift(): return lax.ppermute(x, 'dp', [(i, (i + by) % NDP) for i in range(NDP)])  6.84 us
    pallas_call x1, Pallas kernels, image_out(): pl.pallas_call(image_kernel, out_shape=jax.ShapeDtypeStruct((NDP, SLOTS,...  6.47 us
    pallas_call x1, Pallas kernels, mix(): pl.pallas_call(mixed_kernel, out_shape=(jax.ShapeDtypeStruct((8, 128), f3...  5.39 us
  transfers between devices with their start and end apart: 16, of which 8 were waited for; matrix products, arithmetic and copies ran while one was open for 2% of the time, Pallas kernels for 15%

profile of v1, /device:TPU:0, one launch (start us, length us, event | category | flops | bytes accessed | tf_op | source)
XLA Modules:
  0.0 128.6 jit_solution(10001132955483993281)
XLA Ops:
  0.6 1.9 %pack_kv.1 = bf16[8,128,256]{2,1,0:T(8,128)(2,1)} custom-call(s32[1]{0:T(128)} %bitcast.half_ref, bf16[128,1024]{1,0:T(8,128)(2,1)} %bitcast.13, bf16[128,1024]{1,0:T(8,128)(2,1)} %bitcast.14), custom_call_target="tpu_custom_call" | custom-call | bytes 6000000 | tf_op jit(solution)/shard_map/pack_kv/pallas_call | solution.py:65
  2.6 5.9 %all-to-all-start.1 = ((bf16[8,128,256]{2,1,0:T(8,128)(2,1)}), bf16[8,128,256]{2,1,0:T(8,128)(2,1)S(1)}, u32[]{:S(2)}, u32[]{:S(2)}) async-start(bf16[8,128,256]{2,1,0:T(8,128)(2,1)} %pack_kv.1), calls=%async_computation.1 | async-start | bytes 1048576 | tf_op jit(solution)/shard_map/all_to_all | solution.py:469
  11.2 2.3 %pack_qd.1.refs_2_ = bf16[8,128,512]{2,1,0:T(8,128)(2,1)} custom-call(s32[1]{0:T(128)} %bitcast.half_ref, bf16[128,2048]{1,0:T(8,128)(2,1)} %bitcast.11, bf16[128,2048]{1,0:T(8,128)(2,1)} %bitcast.12), custom_call_target="tpu_custom_call" | custom-call | bytes 6000000 | tf_op jit(solution)/shard_map/pack_qd/pallas_call | solution.py:65
  14.1 5.4 %mix.1 = (f32[8,128]{1,0:T(8,128)}, bf16[64,2176]{1,0:T(8,128)(2,1)}, bf16[64,2176]{1,0:T(8,128)(2,1)}, bf16[64,2176]{1,0:T(8,128)(2,1)}, bf16[64,2176]{1,0:T(8,128)(2,1)}) custom-call(s32[6]{0:T(128)} %stack.16.sc_ref, s32[4]{0:T(128)} %dynamic_slice.3.owner_ref, bf16[4,64,1152]{2,1,0:T(8,128)(2,1)} %embed_ref.3, f32[1152]{0:T(1024)} %scale_ref.3, ...), custom_call_target="tpu_custom_call" | custom-call | bytes 15000000 | tf_op jit(solution)/shard_map/mix/pallas_call | solution.py:110
  20.2 4.1 %collective-permute-start.1 = (bf16[8,128,256]{2,1,0:T(8,128)(2,1)S(1)}, bf16[8,128,256]{2,1,0:T(8,128)(2,1)S(1)}, u32[]{:S(2)}, u32[]{:S(2)}) collective-permute-start(bf16[8,128,256]{2,1,0:T(8,128)(2,1)S(1)} %join.2.kv0_ref), channel_id=1, source_target_pairs={{0,6},{2,4},{4,2},{6,0},{1,7},{3,5},{5,3},{7,1},{8,14},{10,12},{12... | collective-permute-start | bytes 1572872 | tf_op jit(solution)/shard_map/ppermute | solution.py:477
  24.3 4.2 %all-to-all-start = ((bf16[8,128,512]{2,1,0:T(8,128)(2,1)}), bf16[8,128,512]{2,1,0:T(8,128)(2,1)S(1)}, u32[]{:S(2)}, u32[]{:S(2)}) async-start(bf16[8,128,512]{2,1,0:T(8,128)(2,1)} %pack_qd.1.refs_2_), calls=%async_computation | async-start | bytes 2097152 | tf_op jit(solution)/shard_map/all_to_all | solution.py:469
  28.6 1.5 %collective-permute-start.2 = (bf16[64,2176]{1,0:T(8,128)(2,1)}, bf16[64,2176]{1,0:T(8,128)(2,1)S(1)}, u32[]{:S(2)}, u32[]{:S(2)}) collective-permute-start(bf16[64,2176]{1,0:T(8,128)(2,1)} %get-tuple-element.19), channel_id=1, source_target_pairs={{0,32},{32,64},{64,96},{96,0},{1,33},{33,65},{65,97},{97,1},{2,34}... | collective-permute-start | bytes 835592 | tf_op jit(solution)/shard_map/ppermute | solution.py:473
  30.1 1.7 %collective-permute-start.3 = (bf16[64,2176]{1,0:T(8,128)(2,1)}, bf16[64,2176]{1,0:T(8,128)(2,1)S(1)}, u32[]{:S(2)}, u32[]{:S(2)}) collective-permute-start(bf16[64,2176]{1,0:T(8,128)(2,1)} %get-tuple-element.20), channel_id=1, source_target_pairs={{0,96},{32,0},{64,32},{96,64},{1,97},{33,1},{65,33},{97,65},{2,98}... | collective-permute-start | bytes 835592 | tf_op jit(solution)/shard_map/ppermute | solution.py:473
  31.8 5.5 %collective-permute-done.2.refs_1_.u1 = bf16[64,2176]{1,0:T(8,128)(2,1)S(1)} collective-permute-done((bf16[64,2176]{1,0:T(8,128)(2,1)}, bf16[64,2176]{1,0:T(8,128)(2,1)S(1)}, u32[]{:S(2)}, u32[]{:S(2)}) %collective-permute-start.2) | collective-permute-done | bytes 278560 | tf_op jit(solution)/shard_map/ppermute | solution.py:473
  37.4 5.9 %all-to-all-done.qd_ref = bf16[8,128,512]{2,1,0:T(8,128)(2,1)S(1)} async-done(((bf16[8,128,512]{2,1,0:T(8,128)(2,1)}), bf16[8,128,512]{2,1,0:T(8,128)(2,1)S(1)}, u32[]{:S(2)}, u32[]{:S(2)}) %all-to-all-start) | async-done | bytes 1048608 | tf_op jit(solution)/shard_map/all_to_all | solution.py:469
  44.5 30.3 %attention.1 = (bf16[8,128,256]{2,1,0:T(8,128)(2,1)}, f32[8,128,256]{2,1,0:T(8,128)}, bf16[8,128,256]{2,1,0:T(8,128)(2,1)}, bf16[8,128,256]{2,1,0:T(8,128)(2,1)}...) custom-call(s32[6]{0:T(128)} %stack.16.sc_ref, bf16[8,128,512]{2,1,0:T(8,128)(2,1)} %copy-done.8, ...), custom_call_target="tpu_custom_call" | custom-call | bytes 108000000 | tf_op jit(solution)/shard_map/attention/pallas_call | solution.py:287
  74.8 4.8 %all-to-all-start.3 = ((bf16[32,64,256]{2,1,0:T(8,128)(2,1)}), bf16[32,64,256]{2,1,0:T(8,128)(2,1)}, u32[]{:S(2)}, u32[]{:S(2)}) async-start(bf16[32,64,256]{2,1,0:T(8,128)(2,1)} %get-tuple-element.29), calls=%async_computation.3 | async-start | bytes 2097152 | tf_op jit(solution)/shard_map/all_to_all | solution.py:469
  82.0 2.8 %collective-permute-start.7 = (bf16[8,128,256]{2,1,0:T(8,128)(2,1)}, bf16[8,128,256]{2,1,0:T(8,128)(2,1)S(1)}, u32[]{:S(2)}, u32[]{:S(2)}) collective-permute-start(bf16[8,128,256]{2,1,0:T(8,128)(2,1)} %pair_sum.1), channel_id=1, source_target_pairs={{0,6},{2,4},{4,2},{6,0},{1,7},{3,5},{5,3},{7,1},{8,14},{10,12},{12... | collective-permute-start | bytes 1572872 | tf_op jit(solution)/shard_map/ppermute | solution.py:477
  84.8 5.3 %collective-permute-done.8.u2 = bf16[64,2176]{1,0:T(8,128)(2,1)S(1)} collective-permute-done((bf16[64,2176]{1,0:T(8,128)(2,1)}, bf16[64,2176]{1,0:T(8,128)(2,1)S(1)}, u32[]{:S(2)}, u32[]{:S(2)}) %collective-permute-start.8) | collective-permute-done | bytes 278560 | tf_op jit(solution)/shard_map/ppermute | solution.py:473
  90.2 6.3 %all-to-all-done.3.tok_ref = bf16[32,64,256]{2,1,0:T(8,128)(2,1)} async-done(((bf16[32,64,256]{2,1,0:T(8,128)(2,1)}), bf16[32,64,256]{2,1,0:T(8,128)(2,1)}, u32[]{:S(2)}, u32[]{:S(2)}) %all-to-all-start.3) | async-done | bytes 1048608 | tf_op jit(solution)/shard_map/all_to_all | solution.py:469
  96.4 2.7 %token_rows.1.r0 = bf16[64,2176]{1,0:T(8,128)(2,1)} custom-call(s32[6]{0:T(128)} %stack.16.sc_ref, bf16[32,64,256]{2,1,0:T(8,128)(2,1)} %all-to-all-done.3.tok_ref, bf16[64,2176]{1,0:T(8,128)(2,1)} %get-tuple-element.30.u0, bf16[64,2176]{1,0:T(8,128)(2,1)} %copy-done.2, bf16[64,2176]{1,0:T(8,128)(2,1)} %copy-done.10, bf16[64,2176]{1,0:T(8,128)(2,1)} %copy-done.3), custom_call_target="tpu_custom_call" | custom-call | bytes 6000000 | tf_op jit(solution)/shard_map/token_rows/pallas_call | solution.py:410
  99.1 1.5 %collective-permute-start.10 = (bf16[64,2176]{1,0:T(8,128)(2,1)}, bf16[64,2176]{1,0:T(8,128)(2,1)}, u32[]{:S(2)}, u32[]{:S(2)}) collective-permute-start(bf16[64,2176]{1,0:T(8,128)(2,1)} %token_rows.1.r0), channel_id=1, source_target_pairs={{0,64},{32,96},{64,0},{96,32},{1,65},{33,97},{65,1},{97,33},{2,66}... | collective-permute-start | bytes 835592 | tf_op jit(solution)/shard_map/ppermute | solution.py:473
  100.6 1.8 %collective-permute-start.9 = (bf16[64,2176]{1,0:T(8,128)(2,1)}, bf16[64,2176]{1,0:T(8,128)(2,1)}, u32[]{:S(2)}, u32[]{:S(2)}) collective-permute-start(bf16[64,2176]{1,0:T(8,128)(2,1)} %token_rows.1.r0), channel_id=1, source_target_pairs={{0,96},{32,0},{64,32},{96,64},{1,97},{33,1},{65,33},{97,65},{2,98}... | collective-permute-start | bytes 835592 | tf_op jit(solution)/shard_map/ppermute | solution.py:473
  102.4 3.6 %collective-permute-done.7.c_ref = bf16[8,128,256]{2,1,0:T(8,128)(2,1)S(1)} collective-permute-done((bf16[8,128,256]{2,1,0:T(8,128)(2,1)}, bf16[8,128,256]{2,1,0:T(8,128)(2,1)S(1)}, u32[]{:S(2)}, u32[]{:S(2)}) %collective-permute-start.7) | collective-permute-done | bytes 524320 | tf_op jit(solution)/shard_map/ppermute | solution.py:477
  106.0 1.2 last_sum.1
  107.2 4.4 %all-to-all-start.2 = ((bf16[8,128,512]{2,1,0:T(8,128)(2,1)}), bf16[8,128,512]{2,1,0:T(8,128)(2,1)S(1)}, u32[]{:S(2)}, u32[]{:S(2)}) async-start(bf16[8,128,512]{2,1,0:T(8,128)(2,1)} %last_sum.1), calls=%async_computation.2 | async-start | bytes 2097152 | tf_op jit(solution)/shard_map/all_to_all | solution.py:469
  111.6 3.9 %collective-permute-done.11.r3 = bf16[64,2176]{1,0:T(8,128)(2,1)S(1)} collective-permute-done((bf16[64,2176]{1,0:T(8,128)(2,1)}, bf16[64,2176]{1,0:T(8,128)(2,1)S(1)}, u32[]{:S(2)}, u32[]{:S(2)}) %collective-permute-start.11) | collective-permute-done | bytes 278560 | tf_op jit(solution)/shard_map/ppermute | solution.py:473
  116.2 6.5 %image_out.1 = f32[4,64,1152]{2,1,0:T(8,128)} custom-call(s32[6]{0:T(128)} %stack.16.sc_ref, s32[4]{0:T(128)} %dynamic_slice.3.owner_ref, bf16[64,2176]{1,0:T(8,128)(2,1)} %token_rows.1.r0, bf16[64,2176]{1,0:T(8,128)(2,1)} %collective-permute-done.9.r1, bf16[64,2176]{1,0:T(8,128)(2,1)} %collective-permute-done.10.r2, bf16[64,2176]{1,0:T(8,128)(2,1)} %copy-done.11, ...), custom_call_target="tpu_custom_call" | custom-call | flops 60000002048 | bytes 15000000 | tf_op jit(solution)/shard_map/image_out/pallas_call | solution.py:452
  122.6 4.8 %all-to-all-done.2.in_ref = bf16[8,128,512]{2,1,0:T(8,128)(2,1)S(1)} async-done(((bf16[8,128,512]{2,1,0:T(8,128)(2,1)}), bf16[8,128,512]{2,1,0:T(8,128)(2,1)S(1)}, u32[]{:S(2)}, u32[]{:S(2)}) %all-to-all-start.2) | async-done | bytes 1048608 | tf_op jit(solution)/shard_map/all_to_all | solution.py:469
  (46 shorter events, 8.3 us)
Async XLA Ops:
  2.6 16.9 %all-to-all-start.1 = ((bf16[8,128,256]{2,1,0:T(8,128)(2,1)}), bf16[8,128,256]{2,1,0:T(8,128)(2,1)S(1)}, u32[]{:S(2)}, u32[]{:S(2)}) async-start(bf16[8,128,256]{2,1,0:T(8,128)(2,1)} %pack_kv.1), calls=%async_computation.1 | async-start | bytes 1048576 | tf_op jit(solution)/shard_map/all_to_all | solution.py:469
  20.2 23.1 %copy-start = (bf16[8,128,256]{2,1,0:T(8,128)(2,1)}, bf16[8,128,256]{2,1,0:T(8,128)(2,1)S(1)}, u32[]{:S(2)}) copy-start(bf16[8,128,256]{2,1,0:T(8,128)(2,1)S(1)} %join.2.kv0_ref) | copy-start | bytes 1572868
  20.2 17.1 %collective-permute-start.1 = (bf16[8,128,256]{2,1,0:T(8,128)(2,1)S(1)}, bf16[8,128,256]{2,1,0:T(8,128)(2,1)S(1)}, u32[]{:S(2)}, u32[]{:S(2)}) collective-permute-start(bf16[8,128,256]{2,1,0:T(8,128)(2,1)S(1)} %join.2.kv0_ref), channel_id=1, source_target_pairs={{0,6},{2,4},{4,2},{6,0},{1,7},{3,5},{5,3},{7,1},{8,14},{10,12},{12... | collective-permute-start | bytes 1572872 | tf_op jit(solution)/shard_map/ppermute | solution.py:477
  24.3 19.0 %all-to-all-start = ((bf16[8,128,512]{2,1,0:T(8,128)(2,1)}), bf16[8,128,512]{2,1,0:T(8,128)(2,1)S(1)}, u32[]{:S(2)}, u32[]{:S(2)}) async-start(bf16[8,128,512]{2,1,0:T(8,128)(2,1)} %pack_qd.1.refs_2_), calls=%async_computation | async-start | bytes 2097152 | tf_op jit(solution)/shard_map/all_to_all | solution.py:469
  28.6 8.7 %collective-permute-start.2 = (bf16[64,2176]{1,0:T(8,128)(2,1)}, bf16[64,2176]{1,0:T(8,128)(2,1)S(1)}, u32[]{:S(2)}, u32[]{:S(2)}) collective-permute-start(bf16[64,2176]{1,0:T(8,128)(2,1)} %get-tuple-element.19), channel_id=1, source_target_pairs={{0,32},{32,64},{64,96},{96,0},{1,33},{33,65},{65,97},{97,1},{2,34}... | collective-permute-start | bytes 835592 | tf_op jit(solution)/shard_map/ppermute | solution.py:473
  30.1 7.2 %collective-permute-start.3 = (bf16[64,2176]{1,0:T(8,128)(2,1)}, bf16[64,2176]{1,0:T(8,128)(2,1)S(1)}, u32[]{:S(2)}, u32[]{:S(2)}) collective-permute-start(bf16[64,2176]{1,0:T(8,128)(2,1)} %get-tuple-element.20), channel_id=1, source_target_pairs={{0,96},{32,0},{64,32},{96,64},{1,97},{33,1},{65,33},{97,65},{2,98}... | collective-permute-start | bytes 835592 | tf_op jit(solution)/shard_map/ppermute | solution.py:473
  31.8 11.5 %collective-permute-start = (bf16[8,128,256]{2,1,0:T(8,128)(2,1)S(1)}, bf16[8,128,256]{2,1,0:T(8,128)(2,1)S(1)}, u32[]{:S(2)}, u32[]{:S(2)}) collective-permute-start(bf16[8,128,256]{2,1,0:T(8,128)(2,1)S(1)} %join.2.kv0_ref), channel_id=1, source_target_pairs={{0,1},{1,0},{2,3},{3,2},{4,5},{5,4},{6,7},{7,6},{8,9},{9,8},{10,11... | collective-permute-start | bytes 1572872 | tf_op jit(solution)/shard_map/ppermute | solution.py:481
  37.3 59.2 %copy-start.2 = (bf16[64,2176]{1,0:T(8,128)(2,1)}, bf16[64,2176]{1,0:T(8,128)(2,1)S(1)}, u32[]{:S(2)}) copy-start(bf16[64,2176]{1,0:T(8,128)(2,1)S(1)} %collective-permute-done.2.refs_1_.u1) | copy-start | bytes 835588
  37.3 59.2 %copy-start.3 = (bf16[64,2176]{1,0:T(8,128)(2,1)}, bf16[64,2176]{1,0:T(8,128)(2,1)S(1)}, u32[]{:S(2)}) copy-start(bf16[64,2176]{1,0:T(8,128)(2,1)S(1)} %collective-permute-done.3.refs_2_.u3) | copy-start | bytes 835588
  37.3 6.0 %copy-start.1 = (bf16[8,128,256]{2,1,0:T(8,128)(2,1)}, bf16[8,128,256]{2,1,0:T(8,128)(2,1)S(1)}, u32[]{:S(2)}) copy-start(bf16[8,128,256]{2,1,0:T(8,128)(2,1)S(1)} %join.3.kv2_ref) | copy-start | bytes 1572868
  37.3 6.0 %collective-permute-start.4 = (bf16[8,128,256]{2,1,0:T(8,128)(2,1)S(1)}, bf16[8,128,256]{2,1,0:T(8,128)(2,1)}, u32[]{:S(2)}, u32[]{:S(2)}) collective-permute-start(bf16[8,128,256]{2,1,0:T(8,128)(2,1)S(1)} %join.3.kv2_ref), channel_id=1, source_target_pairs={{0,1},{1,0},{2,3},{3,2},{4,5},{5,4},{6,7},{7,6},{8,9},{9,8},{10,11... | collective-permute-start | bytes 1572872 | tf_op jit(solution)/shard_map/ppermute | solution.py:481
  43.3 1.1 copy-start.9
  74.7 31.2 %copy-start.4 = (f32[8,128,256]{2,1,0:T(8,128)S(1)}, f32[8,128,256]{2,1,0:T(8,128)}, u32[]{:S(2)}) copy-start(f32[8,128,256]{2,1,0:T(8,128)} %get-tuple-element.22.a_ref) | copy-start | bytes 3145732
  74.8 31.2 %copy-start.5 = (bf16[8,128,256]{2,1,0:T(8,128)(2,1)S(1)}, bf16[8,128,256]{2,1,0:T(8,128)(2,1)}, u32[]{:S(2)}) copy-start(bf16[8,128,256]{2,1,0:T(8,128)(2,1)} %get-tuple-element.21.dq_ref) | copy-start | bytes 1572868
  74.8 5.3 %collective-permute-start.6 = (bf16[8,128,256]{2,1,0:T(8,128)(2,1)}, bf16[8,128,256]{2,1,0:T(8,128)(2,1)S(1)}, u32[]{:S(2)}, u32[]{:S(2)}) collective-permute-start(bf16[8,128,256]{2,1,0:T(8,128)(2,1)} %get-tuple-element.25), channel_id=1, source_target_pairs={{0,1},{1,0},{2,3},{3,2},{4,5},{5,4},{6,7},{7,6},{8,9},{9,8},{10,11... | collective-permute-start | bytes 1572872 | tf_op jit(solution)/shard_map/ppermute | solution.py:481
  74.8 21.6 %all-to-all-start.3 = ((bf16[32,64,256]{2,1,0:T(8,128)(2,1)}), bf16[32,64,256]{2,1,0:T(8,128)(2,1)}, u32[]{:S(2)}, u32[]{:S(2)}) async-start(bf16[32,64,256]{2,1,0:T(8,128)(2,1)} %get-tuple-element.29), calls=%async_computation.3 | async-start | bytes 2097152 | tf_op jit(solution)/shard_map/all_to_all | solution.py:469
  79.7 10.5 %collective-permute-start.8 = (bf16[64,2176]{1,0:T(8,128)(2,1)}, bf16[64,2176]{1,0:T(8,128)(2,1)S(1)}, u32[]{:S(2)}, u32[]{:S(2)}) collective-permute-start(bf16[64,2176]{1,0:T(8,128)(2,1)} %get-tuple-element.31), channel_id=1, source_target_pairs={{0,64},{32,96},{64,0},{96,32},{1,65},{33,97},{65,1},{97,33},{2,66}... | collective-permute-start | bytes 835592 | tf_op jit(solution)/shard_map/ppermute | solution.py:473
  80.0 22.4 %collective-permute-start.5 = (bf16[8,128,256]{2,1,0:T(8,128)(2,1)}, bf16[8,128,256]{2,1,0:T(8,128)(2,1)S(1)}, u32[]{:S(2)}, u32[]{:S(2)}) collective-permute-start(bf16[8,128,256]{2,1,0:T(8,128)(2,1)} %get-tuple-element.23), channel_id=1, source_target_pairs={{0,1},{1,0},{2,3},{3,2},{4,5},{5,4},{6,7},{7,6},{8,9},{9,8},{10,11... | collective-permute-start | bytes 1572872 | tf_op jit(solution)/shard_map/ppermute | solution.py:481
  82.0 24.0 %collective-permute-start.7 = (bf16[8,128,256]{2,1,0:T(8,128)(2,1)}, bf16[8,128,256]{2,1,0:T(8,128)(2,1)S(1)}, u32[]{:S(2)}, u32[]{:S(2)}) collective-permute-start(bf16[8,128,256]{2,1,0:T(8,128)(2,1)} %pair_sum.1), channel_id=1, source_target_pairs={{0,6},{2,4},{4,2},{6,0},{1,7},{3,5},{5,3},{7,1},{8,14},{10,12},{12... | collective-permute-start | bytes 1572872 | tf_op jit(solution)/shard_map/ppermute | solution.py:477
  90.2 6.3 %copy-start.10 = (bf16[64,2176]{1,0:T(8,128)(2,1)}, bf16[64,2176]{1,0:T(8,128)(2,1)S(1)}, u32[]{:S(2)}) copy-start(bf16[64,2176]{1,0:T(8,128)(2,1)S(1)} %collective-permute-done.8.u2) | copy-start | bytes 835588
  99.1 16.3 %collective-permute-start.11 = (bf16[64,2176]{1,0:T(8,128)(2,1)}, bf16[64,2176]{1,0:T(8,128)(2,1)S(1)}, u32[]{:S(2)}, u32[]{:S(2)}) collective-permute-start(bf16[64,2176]{1,0:T(8,128)(2,1)} %token_rows.1.r0), channel_id=1, source_target_pairs={{0,32},{32,64},{64,96},{96,0},{1,33},{33,65},{65,97},{97,1},{2,34}... | collective-permute-start | bytes 835592 | tf_op jit(solution)/shard_map/ppermute | solution.py:473
  99.1 16.3 %collective-permute-start.10 = (bf16[64,2176]{1,0:T(8,128)(2,1)}, bf16[64,2176]{1,0:T(8,128)(2,1)}, u32[]{:S(2)}, u32[]{:S(2)}) collective-permute-start(bf16[64,2176]{1,0:T(8,128)(2,1)} %token_rows.1.r0), channel_id=1, source_target_pairs={{0,64},{32,96},{64,0},{96,32},{1,65},{33,97},{65,1},{97,33},{2,66}... | collective-permute-start | bytes 835592 | tf_op jit(solution)/shard_map/ppermute | solution.py:473
  100.6 15.6 %collective-permute-start.9 = (bf16[64,2176]{1,0:T(8,128)(2,1)}, bf16[64,2176]{1,0:T(8,128)(2,1)}, u32[]{:S(2)}, u32[]{:S(2)}) collective-permute-start(bf16[64,2176]{1,0:T(8,128)(2,1)} %token_rows.1.r0), channel_id=1, source_target_pairs={{0,96},{32,0},{64,32},{96,64},{1,97},{33,1},{65,33},{97,65},{2,98}... | collective-permute-start | bytes 835592 | tf_op jit(solution)/shard_map/ppermute | solution.py:473
  107.2 20.3 %all-to-all-start.2 = ((bf16[8,128,512]{2,1,0:T(8,128)(2,1)}), bf16[8,128,512]{2,1,0:T(8,128)(2,1)S(1)}, u32[]{:S(2)}, u32[]{:S(2)}) async-start(bf16[8,128,512]{2,1,0:T(8,128)(2,1)} %last_sum.1), calls=%async_computation.2 | async-start | bytes 2097152 | tf_op jit(solution)/shard_map/all_to_all | solution.py:469
  (4 other events, 3.4 us)
